TPU v7x, 128 devices: a whole 4x4x4 slice. The times are simulated.
128 devices in a mesh: row: 16 (over z, x), col: 8 (over y, core).
Axes of the slice: x: 4, y: 4, z: 4, core: 2. Of those that a mesh axis runs over, the one named last changes fastest.
Arguments:
- targets: float32 [10, 1024, 1024], P(None, 'row', 'col'), may hold values from -6 to 6
- lower_panel: float32 [10, 1024, 29696], P(None, 'row', 'col'), may hold values from -0.03125 to 0.03125
- prior_solution: float32 [29696, 1024], P('col', 'row'), may hold values from -6 to 6
- diag_inverse: float32 [10, 1024, 1024], P(None, 'row'), may hold values from -2 to 2, as said below
- below_blocks: float32 [45, 1024, 1024], P(None, 'row'), may hold values from -0.1875 to 0.1875
Outputs:
- solution: float32 [10, 1024, 1024], P(None, 'row', 'col')
Inputs may be any that keep to these rules, and one draw needn't show every extreme that they name: `diag_inverse`: each block is lower triangular with a positive diagonal.
All inputs are finite; a program needn't handle non-finite values.
Results may differ from a plain program's by a relative error of at most 0.00019.
Values sent between devices are 32-bit elements; how exact they have to be, the bound alone decides.
A program may use at most 192 MiB of HBM per device.

v0:
```python
import jax
import jax.numpy as jnp
from jax import lax
from jax.sharding import PartitionSpec as P


def product(left, right):
    return jnp.dot(left, right, precision=lax.Precision.HIGHEST, preferred_element_type=jnp.float32)


def on_device(targets, lower_panel, prior_solution, diag_inverse, below_blocks):
    step_count, row_count, prior_width = lower_panel.shape
    flattened = lower_panel.reshape(step_count * row_count, prior_width)
    partial_value = product(flattened, lax.all_gather(prior_solution, "row", axis=1, tiled=True))
    reduced = lax.psum_scatter(partial_value, "col", scatter_dimension=1, tiled=True).reshape(
        step_count, row_count, -1
    )
    earlier = [reduced[k] for k in range(step_count)]
    solved = []
    outputs = []
    for k in range(step_count):
        remainder = targets[k] - earlier[k]
        for j in range(k):
            remainder = remainder - product(below_blocks[k * (k - 1) // 2 + j], solved[j])
        gathered = lax.all_gather(remainder, "row", axis=0, tiled=True)
        own_rows = product(diag_inverse[k], gathered)
        outputs.append(own_rows)
        if k + 1 < step_count:
            solved.append(lax.all_gather(own_rows, "row", axis=0, tiled=True))
    return jnp.stack(outputs)


def solution(mesh):
    in_specs = (
        P(None, "row", "col"),
        P(None, "row", "col"),
        P("col", "row"),
        P(None, "row", None),
        P(None, "row", None),
    )
    out_specs = P(None, "row", "col")
    return jax.shard_map(
        on_device, mesh=mesh, in_specs=in_specs, out_specs=out_specs, check_vma=False
    )
```

profile of v0, /device:TPU:24, one launch (start us, length us, event | category | flops | bytes accessed | tf_op | source)
XLA Modules:
  0.0 665.9 jit_solution(5472094716047747026)
XLA Ops:
  7.3 107.8 %all-gather.2.cloned.1.call-done = f32[3712,1024]{0,1:T(8,128)} async-done(((f32[3712,64]{0,1:T(8,128)}), f32[3712,1024]{0,1:T(8,128)}) %all-gather.2.cloned.1.call-update) | async-done | bytes 15204368 | tf_op jit(solution)/shard_map/all_gather | solution.py:14
  115.1 36.3 %fusion.165 = f32[640,1024]{1,0:T(8,128)} fusion(f32[640,3712]{1,0:T(8,128)} %bitcast.494, f32[3712,1024]{0,1:T(8,128)} %all-gather.2.cloned.1.call-done), kind=kOutput, calls=%fused_computation.230 | convolution fusion | flops 29192355840 | bytes 27328512 | tf_op jit(solution)/shard_map/dot_general | solution.py:8
  151.4 31.0 %reduce-scatter.2.cloned.1.call-done = f32[640,128]{1,0:T(8,128)} async-done(((f32[640,1024]{1,0:T(8,128)}), f32[640,128]{1,0:T(8,128)}) %reduce-scatter.2.cloned.1.call-update) | async-done | bytes 327696 | tf_op jit(solution)/shard_map/reduce_scatter | solution.py:15
  183.3 24.5 %all_gather.61 = f32[1024,128]{1,0:T(8,128)S(1)} all-gather(f32[64,128]{1,0:T(8,128)S(1)} %slice_subtract_fusion.9), channel_id=1, replica_groups=mesh['row'=16,'col'=8] {'row'}, dimensions={0}, use_global_device_ids=true | all-gather | bytes 557056 | tf_op jit(solution)/shard_map/all_gather | solution.py:25
  209.2 23.2 %all_gather.62 = f32[1024,128]{1,0:T(8,128)S(1)} all-gather(f32[64,128]{1,0:T(8,128)S(1)} %bitcast.493), channel_id=1, replica_groups=mesh['row'=16,'col'=8] {'row'}, dimensions={0}, use_global_device_ids=true | all-gather | bytes 557056 | tf_op jit(solution)/shard_map/all_gather | solution.py:29
  232.4 1.4 fusion.45
  233.8 22.1 %all_gather.63 = f32[1024,128]{1,0:T(8,128)S(1)} all-gather(f32[64,128]{1,0:T(8,128)S(1)} %fusion.45), channel_id=1, replica_groups=mesh['row'=16,'col'=8] {'row'}, dimensions={0}, use_global_device_ids=true | all-gather | bytes 557056 | tf_op jit(solution)/shard_map/all_gather | solution.py:25
  257.4 23.1 %all_gather.64 = f32[1024,128]{1,0:T(8,128)S(1)} all-gather(f32[64,128]{1,0:T(8,128)S(1)} %bitcast.485), channel_id=1, replica_groups=mesh['row'=16,'col'=8] {'row'}, dimensions={0}, use_global_device_ids=true | all-gather | bytes 557056 | tf_op jit(solution)/shard_map/all_gather | solution.py:29
  280.5 1.6 fusion.9
  283.5 1.4 fusion.17
  286.3 1.4 fusion.24
  289.1 1.4 fusion.30
  291.9 1.4 fusion.35
  293.3 1.5 fusion.34
  294.9 1.4 fusion.39
  297.7 1.4 fusion.42
  300.5 1.4 fusion.44
  303.3 22.2 %all_gather.65 = f32[1024,128]{1,0:T(8,128)S(1)} all-gather(f32[64,128]{1,0:T(8,128)S(1)} %fusion.43), channel_id=1, replica_groups=mesh['row'=16,'col'=8] {'row'}, dimensions={0}, use_global_device_ids=true | all-gather | bytes 557056 | tf_op jit(solution)/shard_map/all_gather | solution.py:25
  325.9 23.1 %all_gather.66 = f32[1024,128]{1,0:T(8,128)S(1)} all-gather(f32[64,128]{1,0:T(8,128)S(1)} %bitcast.486), channel_id=1, replica_groups=mesh['row'=16,'col'=8] {'row'}, dimensions={0}, use_global_device_ids=true | all-gather | bytes 557056 | tf_op jit(solution)/shard_map/all_gather | solution.py:29
  352.2 22.1 %all_gather.67 = f32[1024,128]{1,0:T(8,128)S(1)} all-gather(f32[64,128]{1,0:T(8,128)S(1)} %fusion.40), channel_id=1, replica_groups=mesh['row'=16,'col'=8] {'row'}, dimensions={0}, use_global_device_ids=true | all-gather | bytes 557056 | tf_op jit(solution)/shard_map/all_gather | solution.py:25
  374.8 23.1 %all_gather.68 = f32[1024,128]{1,0:T(8,128)S(1)} all-gather(f32[64,128]{1,0:T(8,128)S(1)} %bitcast.487), channel_id=1, replica_groups=mesh['row'=16,'col'=8] {'row'}, dimensions={0}, use_global_device_ids=true | all-gather | bytes 557056 | tf_op jit(solution)/shard_map/all_gather | solution.py:29
  400.6 22.0 %all_gather.69 = f32[1024,128]{1,0:T(8,128)S(1)} all-gather(f32[64,128]{1,0:T(8,128)S(1)} %fusion.36), channel_id=1, replica_groups=mesh['row'=16,'col'=8] {'row'}, dimensions={0}, use_global_device_ids=true | all-gather | bytes 557056 | tf_op jit(solution)/shard_map/all_gather | solution.py:25
  423.1 23.2 %all_gather.70 = f32[1024,128]{1,0:T(8,128)S(1)} all-gather(f32[64,128]{1,0:T(8,128)S(1)} %bitcast.488), channel_id=1, replica_groups=mesh['row'=16,'col'=8] {'row'}, dimensions={0}, use_global_device_ids=true | all-gather | bytes 557056 | tf_op jit(solution)/shard_map/all_gather | solution.py:29
  448.5 22.2 %all_gather.71 = f32[1024,128]{1,0:T(8,128)S(1)} all-gather(f32[64,128]{1,0:T(8,128)S(1)} %fusion.31), channel_id=1, replica_groups=mesh['row'=16,'col'=8] {'row'}, dimensions={0}, use_global_device_ids=true | all-gather | bytes 557056 | tf_op jit(solution)/shard_map/all_gather | solution.py:25
  471.1 23.1 %all_gather.72 = f32[1024,128]{1,0:T(8,128)S(1)} all-gather(f32[64,128]{1,0:T(8,128)S(1)} %bitcast.489), channel_id=1, replica_groups=mesh['row'=16,'col'=8] {'row'}, dimensions={0}, use_global_device_ids=true | all-gather | bytes 557056 | tf_op jit(solution)/shard_map/all_gather | solution.py:29
  496.0 22.0 %all_gather.73 = f32[1024,128]{1,0:T(8,128)S(1)} all-gather(f32[64,128]{1,0:T(8,128)S(1)} %fusion.25), channel_id=1, replica_groups=mesh['row'=16,'col'=8] {'row'}, dimensions={0}, use_global_device_ids=true | all-gather | bytes 557056 | tf_op jit(solution)/shard_map/all_gather | solution.py:25
  518.5 23.2 %all_gather.74 = f32[1024,128]{1,0:T(8,128)S(1)} all-gather(f32[64,128]{1,0:T(8,128)S(1)} %bitcast.490), channel_id=1, replica_groups=mesh['row'=16,'col'=8] {'row'}, dimensions={0}, use_global_device_ids=true | all-gather | bytes 557056 | tf_op jit(solution)/shard_map/all_gather | solution.py:29
  543.0 22.1 %all_gather.75 = f32[1024,128]{1,0:T(8,128)S(1)} all-gather(f32[64,128]{1,0:T(8,128)S(1)} %fusion.18), channel_id=1, replica_groups=mesh['row'=16,'col'=8] {'row'}, dimensions={0}, use_global_device_ids=true | all-gather | bytes 557056 | tf_op jit(solution)/shard_map/all_gather | solution.py:25
  565.6 22.9 %all_gather.76 = f32[1024,128]{1,0:T(8,128)S(1)} all-gather(f32[64,128]{1,0:T(8,128)S(1)} %bitcast.491), channel_id=1, replica_groups=mesh['row'=16,'col'=8] {'row'}, dimensions={0}, use_global_device_ids=true | all-gather | bytes 557056 | tf_op jit(solution)/shard_map/all_gather | solution.py:29
  589.4 22.1 %all_gather.77 = f32[1024,128]{1,0:T(8,128)S(1)} all-gather(f32[64,128]{1,0:T(8,128)S(1)} %fusion.10), channel_id=1, replica_groups=mesh['row'=16,'col'=8] {'row'}, dimensions={0}, use_global_device_ids=true | all-gather | bytes 557056 | tf_op jit(solution)/shard_map/all_gather | solution.py:25
  612.0 22.9 %all_gather.78 = f32[1024,128]{1,0:T(8,128)S(1)} all-gather(f32[64,128]{1,0:T(8,128)S(1)} %bitcast.492), channel_id=1, replica_groups=mesh['row'=16,'col'=8] {'row'}, dimensions={0}, use_global_device_ids=true | all-gather | bytes 557056 | tf_op jit(solution)/shard_map/all_gather | solution.py:29
  635.4 22.1 %all_gather.79 = f32[1024,128]{1,0:T(8,128)S(1)} all-gather(f32[64,128]{1,0:T(8,128)S(1)} %fusion.1), channel_id=1, replica_groups=mesh['row'=16,'col'=8] {'row'}, dimensions={0}, use_global_device_ids=true | all-gather | bytes 557056 | tf_op jit(solution)/shard_map/all_gather | solution.py:25
  (61 shorter events, 30.9 us)
Async XLA Ops:
  6.5 108.5 %all-gather.2.cloned.1.call-start = ((), (), s32[]{:S(2)}) async-start(), calls=%async_computation.1 | async-start | bytes 16154624 | tf_op jit(solution)/shard_map/all_gather | solution.py:14
  7.3 175.1 %reduce-scatter.2.cloned.1.call-start = ((), (), s32[]{:S(2)}) async-start(), calls=%async_computation.2 | async-start | bytes 2949120 | tf_op jit(solution)/shard_map/reduce_scatter | solution.py:15
  151.3 197.7 %slice-start = ((s8[11796480]{0:T(1024)(128)(4,1)}), s8[3407872]{0:T(1024)(128)(4,1)S(1)}, s32[]{:S(2)}) async-start(s8[11796480]{0:T(1024)(128)(4,1)} %bitcast.483), calls=%async_computation.3 | async-start | bytes 6815744
  182.4 143.1 %copy-start = (f32[10,64,1024]{2,1,0:T(8,128)S(1)}, f32[10,64,1024]{2,1,0:T(8,128)}, u32[]{:S(2)}) copy-start(f32[10,64,1024]{2,1,0:T(8,128)} %param.8) | copy-start | bytes 7864324
  280.5 68.6 %slice-start.1 = ((s8[11796480]{0:T(1024)(128)(4,1)}), s8[4194304]{0:T(1024)(128)(4,1)S(1)}, s32[]{:S(2)}) async-start(s8[11796480]{0:T(1024)(128)(4,1)} %bitcast.483), calls=%async_computation.4 | async-start | bytes 8388608
  293.3 55.8 %slice-start.2 = ((s8[11796480]{0:T(1024)(128)(4,1)}), s8[4194304]{0:T(1024)(128)(4,1)S(1)}, s32[]{:S(2)}) async-start(s8[11796480]{0:T(1024)(128)(4,1)} %bitcast.483), calls=%async_computation.5 | async-start | bytes 8388608
  612.0 45.5 %copy-start.1 = (f32[10,64,128]{2,1,0:T(8,128)}, f32[10,64,128]{2,1,0:T(8,128)S(1)}, u32[]{:S(2)}) copy-start(f32[10,64,128]{2,1,0:T(8,128)S(1)} %get-tuple-element.21) | copy-start | bytes 983044
Sparse Core Ops, SparseCore 0:
  9.5 105.5 all-gather.1
  151.5 30.8 reduce-scatter.1
where the time goes:
time: 677 us; the launch traced here: 666 us
  blocking collectives  431 us (64%)
  waiting for transfers between devices  140 us (21%)
  matrix products  79.9 us (12%)
  between operations  14.1 us (2%)
    all_gather x10, blocking collectives, on_device(): gathered = lax.all_gather(remainder, 'row', axis=0, tiled=True)  223 us
    all_gather x9, blocking collectives, on_device(): solved.append(lax.all_gather(own_rows, 'row', axis=0, tiled=True))  208 us
    all_gather x1, waiting for transfers between devices, on_device(): lax.all_gather(prior_solution, 'row', axis=1, tiled=True)  108 us
    dot_general x56, matrix products, product(): jnp.dot(left, right, precision=lax.Precision.HIGHEST, preferred_element_t...  79.9 us
    reduce_scatter x1, waiting for transfers between devices, on_device(): lax.psum_scatter(partial_value, 'col', scatter_dimension=1, tiled=True)  31 us
  transfers between devices with their start and end apart: 2, of which 2 were waited for; matrix products, arithmetic and copies ran while one was open for 0% of the time, Pallas kernels for 0%

commit v1 on v0

v1 whole, which is shorter than its diff:
```python
import jax
import jax.numpy as jnp
from jax import lax
from jax.experimental import pallas as pl
from jax.experimental.pallas import tpu as pltpu
from jax.sharding import PartitionSpec as P

MESH = pl.DeviceIdType.MESH
STEPS = 10
ROWS = 16


def product(left, right):
    return jnp.dot(left, right, precision=lax.Precision.HIGHEST, preferred_element_type=jnp.float32)


def split(value):
    high = value.astype(jnp.bfloat16)
    return high, (value - high.astype(jnp.float32)).astype(jnp.bfloat16)


def dot(left, right):
    return jnp.dot(left, right, preferred_element_type=jnp.float32)


def solve_kernel(rhs_ref, diag_ref, coupling_ref, out_ref, held, own, weights, send_sem, recv_sem):
    row = lax.axis_index("row")
    barrier = pltpu.get_barrier_semaphore()
    for d in range(1, ROWS):
        pl.semaphore_signal(barrier, inc=1, device_id={"row": lax.rem(row + d, ROWS)}, device_id_type=MESH)
    pl.semaphore_wait(barrier, ROWS - 1)

    def copy(k, d):
        return pltpu.make_async_remote_copy(
            src_ref=own.at[k],
            dst_ref=held.at[k, row],
            send_sem=send_sem.at[lax.rem(k, 2), d],
            recv_sem=recv_sem.at[lax.rem(k, 2), d],
            device_id={"row": lax.rem(row + d, ROWS)},
            device_id_type=MESH,
        )

    def send(k):
        for d in range(1, ROWS):
            copy(k, d).start()
        held[k, row] = own[k]

    def arrive(k):
        for d in range(1, ROWS):
            copy(k, d).wait_recv()
        high, low = split(held[k].reshape(ROWS * held.shape[2], held.shape[3]))
        weights[...] = jnp.concatenate([high, low], axis=1)

    def times(block):
        high, low = split(block)
        both = dot(high, weights[...])
        return both[:, :128] + both[:, 128:] + dot(low, weights[:, :128])

    def coupling(i, k):
        pair = i * (i - 1) // 2 + k
        return jnp.concatenate([coupling_ref[c, pair] for c in range(8)], axis=1)

    own[...] = rhs_ref[...]
    send(0)

    def step(k, carry):
        arrive(k)
        own[k + 1] -= times(coupling(k + 1, k))
        send(k + 1)
        out_ref[k] = times(diag_ref[k])

        def later(i, carry):
            own[i] -= times(coupling(i, k))
            return carry

        lax.fori_loop(k + 2, STEPS, later, 0)
        for d in range(1, ROWS):
            copy(k, d).wait_send()
        return carry

    lax.fori_loop(0, STEPS - 1, step, 0)
    arrive(STEPS - 1)
    out_ref[STEPS - 1] = times(diag_ref[STEPS - 1])
    for d in range(1, ROWS):
        copy(STEPS - 1, d).wait_send()


def solve(rhs, diag, coupling):
    steps, rows, columns = rhs.shape
    return pl.pallas_call(
        solve_kernel,
        out_shape=jax.ShapeDtypeStruct(rhs.shape, jnp.float32),
        in_specs=[pl.BlockSpec(memory_space=pltpu.VMEM)] * 3,
        out_specs=pl.BlockSpec(memory_space=pltpu.VMEM),
        scratch_shapes=[
            pltpu.VMEM((steps, ROWS, rows, columns), jnp.float32),
            pltpu.VMEM((steps, rows, columns), jnp.float32),
            pltpu.VMEM((ROWS * rows, 2 * columns), jnp.bfloat16),
            pltpu.SemaphoreType.DMA((2, ROWS)),
            pltpu.SemaphoreType.DMA((2, ROWS)),
        ],
        compiler_params=pltpu.CompilerParams(
            collective_id=1, has_side_effects=True, vmem_limit_bytes=48 << 20
        ),
    )(rhs, diag, coupling)


def on_device(targets, lower_panel, prior_solution, diag_inverse, below_blocks):
    step_count, row_count, prior_width = lower_panel.shape
    col = lax.axis_index("col")
    width = diag_inverse.shape[2] // 8
    diag_part = lax.dynamic_slice_in_dim(diag_inverse, col * width, width, 2)
    diag_columns = lax.all_gather(diag_part, "row", axis=1, tiled=True)
    parts = []
    for i in range(1, step_count):
        for j in range(i):
            parts.append(product(below_blocks[i * (i - 1) // 2 + j], diag_columns[j]))
    coupling = lax.all_gather(jnp.stack(parts), "col", axis=0)
    flattened = lower_panel.reshape(step_count * row_count, prior_width)
    partial_value = product(flattened, lax.all_gather(prior_solution, "row", axis=1, tiled=True))
    reduced = lax.psum_scatter(partial_value, "col", scatter_dimension=1, tiled=True).reshape(
        step_count, row_count, -1
    )
    return solve(targets - reduced, diag_inverse, coupling)


def solution(mesh):
    in_specs = (
        P(None, "row", "col"),
        P(None, "row", "col"),
        P("col", "row"),
        P(None, "row", None),
        P(None, "row", None),
    )
    out_specs = P(None, "row", "col")
    return jax.shard_map(
        on_device, mesh=mesh, in_specs=in_specs, out_specs=out_specs, check_vma=False
    )
```

time: 677 us -> 422 us (0.62); the launches traced: 666 us -> 419 us
  blocking collectives: 431 us -> 0 us
  Pallas kernels: 0 us -> 92.4 us
  matrix products: 79.9 us -> 131 us
  waiting for transfers between devices: 140 us -> 178 us
    all_gather x19 -> x0, blocking collectives: 431 us -> none  [the longest x10 223 us: on_device(): gathered = lax.all_gather(remainder, 'row', axis=0, tiled=True)]
    all_gather x0 -> x2, waiting for transfers between devices: none -> 120 us  [the longest x1 60.9 us: on_device(): coupling = lax.all_gather(jnp.stack(parts), 'col', axis=0)]
    pallas_call x0 -> x1, Pallas kernels: none -> 92.4 us  [solve(): pl.pallas_call(solve_kernel, out_shape=jax.ShapeDtypeStruct(rhs.shape, jn...]
    dot_general x56 -> x46, matrix products: 79.9 us -> 131 us  [product(): jnp.dot(left, right, precision=lax.Precision.HIGHEST, preferred_element_t...]
    all_gather x1, waiting for transfers between devices: 108 us -> 57.7 us  [on_device(): lax.all_gather(prior_solution, 'row', axis=1, tiled=True)]
    reduce_scatter x1, waiting for transfers between devices: 31 us -> 0.02 us  [on_device(): lax.psum_scatter(partial_value, 'col', scatter_dimension=1, tiled=True)]
  transfers between devices with their start and end apart: 2 -> 4, of which waited for: 2 -> 3; matrix products, arithmetic and copies ran while one was open for 0% -> 23% of each run, Pallas kernels for 0% -> 0%
where the time goes in v1:
time: 422 us; the launch traced here: 419 us
  waiting for transfers between devices  178 us (42%)
  matrix products  131 us (31%)
  Pallas kernels  92.4 us (22%)
  between operations  13.2 us (3%)
    dot_general x46, matrix products, product(): jnp.dot(left, right, precision=lax.Precision.HIGHEST, preferred_element_t...  131 us
    pallas_call x1, Pallas kernels, solve(): pl.pallas_call(solve_kernel, out_shape=jax.ShapeDtypeStruct(rhs.shape, jn...  92.4 us
    all_gather x1, waiting for transfers between devices, on_device(): coupling = lax.all_gather(jnp.stack(parts), 'col', axis=0)  60.9 us
    all_gather x1, waiting for transfers between devices, on_device(): diag_columns = lax.all_gather(diag_part, 'row', axis=1, tiled=True)  59 us
    all_gather x1, waiting for transfers between devices, on_device(): lax.all_gather(prior_solution, 'row', axis=1, tiled=True)  57.7 us
  transfers between devices with their start and end apart: 4, of which 3 were waited for; matrix products, arithmetic and copies ran while one was open for 23% of the time, Pallas kernels for 0%

profile of v1, /device:TPU:24, one launch (start us, length us, event | category | flops | bytes accessed | tf_op | source)
XLA Modules:
  0.0 419.1 jit_solution(13251454271975981974)
XLA Ops:
  9.1 59.0 %all-gather.7.cloned.1.call-done = f32[10,1024,128]{2,1,0:T(8,128)} async-done(((f32[10,64,128]{2,1,0:T(8,128)}), f32[10,1024,128]{2,1,0:T(8,128)}) %all-gather.7.cloned.1.call-update) | async-done | bytes 5242896 | tf_op jit(solution)/shard_map/all_gather | solution.py:113
  68.1 2.3 fusion.44
  70.4 2.1 fusion.43
  76.8 2.1 fusion.40
  79.0 2.2 fusion.39
  81.2 2.3 fusion.38
  115.6 57.7 %all-gather.5.cloned.1.call-done = f32[3712,1024]{0,1:T(8,128)} async-done(((f32[3712,64]{0,1:T(8,128)}), f32[3712,1024]{0,1:T(8,128)}) %all-gather.5.cloned.1.call-update) | async-done | bytes 15204368 | tf_op jit(solution)/shard_map/all_gather | solution.py:120
  173.3 36.3 %fusion.135 = f32[640,1024]{1,0:T(8,128)} fusion(f32[640,3712]{1,0:T(8,128)} %bitcast.475, f32[3712,1024]{0,1:T(8,128)} %all-gather.5.cloned.1.call-done), kind=kOutput, calls=%fused_computation.190 | convolution fusion | flops 29192355840 | bytes 27328512 | tf_op jit(solution)/shard_map/dot_general | solution.py:14
  209.9 2.2 fusion.21
  212.0 2.1 fusion.20
  214.2 2.2 fusion.19
  216.3 2.1 fusion.18
  218.5 2.2 fusion.17
  220.6 2.2 fusion.16
  222.8 2.1 fusion.15
  225.0 2.2 fusion.14
  227.1 2.2 fusion.13
  229.3 2.2 fusion.12
  231.4 2.2 fusion.11
  233.6 2.2 fusion.10
  235.8 2.3 fusion.9
  238.1 2.2 fusion.8
  240.3 2.2 fusion.7
  242.4 2.1 fusion.6
  244.6 2.1 fusion.5
  246.7 2.2 fusion.4
  248.9 2.1 fusion.3
  251.0 2.2 fusion.2
  253.2 2.1 fusion.1
  255.3 2.1 fusion
  258.5 60.9 %all-gather.9.cloned.1.call-done = f32[360,64,128]{2,1,0:T(8,128)} async-done(((f32[45,64,128]{2,1,0:T(8,128)}), f32[360,64,128]{2,1,0:T(8,128)}) %all-gather.9.cloned.1.call-update) | async-done | bytes 11796496 | tf_op jit(solution)/shard_map/all_gather | solution.py:118
  319.4 92.4 %shard_map.55 = f32[10,64,128]{2,1,0:T(8,128)S(1)} custom-call(f32[10,64,128]{2,1,0:T(8,128)S(1)} %sub.3.rhs_ref, f32[10,64,1024]{2,1,0:T(8,128)S(1)} %copy-done, f32[8,45,64,128]{3,2,1,0:T(8,128)} %bitcast.473), custom_call_target="tpu_custom_call" | custom-call | tf_op jit(solution)/shard_map/pallas_call | solution.py:90
  (36 shorter events, 40.9 us)
Async XLA Ops:
  6.5 61.6 %all-gather.7.cloned.1.call-start = ((), (), s32[]{:S(2)}) async-start(), calls=%async_computation.3 | async-start | bytes 5570560 | tf_op jit(solution)/shard_map/all_gather | solution.py:113
  8.3 165.0 %all-gather.5.cloned.1.call-start = ((), (), s32[]{:S(2)}) async-start(), calls=%async_computation.1 | async-start | bytes 16154624 | tf_op jit(solution)/shard_map/all_gather | solution.py:120
  9.0 248.5 %reduce-scatter.2.cloned.1.call-start = ((), (), s32[]{:S(2)}) async-start(), calls=%async_computation.2 | async-start | bytes 2949120 | tf_op jit(solution)/shard_map/reduce_scatter | solution.py:121
  68.1 15.4 %copy-start.1 = (f32[10,1024,128]{2,1,0:T(8,128)S(1)}, f32[10,1024,128]{2,1,0:T(8,128)}, u32[]{:S(2)}) copy-start(f32[10,1024,128]{2,1,0:T(8,128)} %all-gather.7.cloned.1.call-done) | copy-start | bytes 15728644
  209.6 109.8 %all-gather.9.cloned.1.call-start = ((), (), s32[]{:S(2)}) async-start(), calls=%async_computation.4 | async-start | bytes 13271040 | tf_op jit(solution)/shard_map/all_gather | solution.py:118
  233.6 23.9 %copy-start.2 = (f32[10,64,128]{2,1,0:T(8,128)S(1)}, f32[10,64,128]{2,1,0:T(8,128)}, u32[]{:S(2)}) copy-start(f32[10,64,128]{2,1,0:T(8,128)} %param.5) | copy-start | bytes 983044
  235.8 83.6 %copy-start = (f32[10,64,1024]{2,1,0:T(8,128)S(1)}, f32[10,64,1024]{2,1,0:T(8,128)}, u32[]{:S(2)}) copy-start(f32[10,64,1024]{2,1,0:T(8,128)} %diag_ref.1) | copy-start | bytes 7864324
Sparse Core Ops, SparseCore 0:
  9.5 58.5 all-gather.6
  70.3 102.9 all-gather.4
  209.7 30.8 reduce-scatter.1
  257.6 61.7 all-gather.8

commit v2 on v1

v2 whole, which is shorter than its diff:
```python
import jax
import jax.numpy as jnp
from jax import lax
from jax.experimental import pallas as pl
from jax.experimental.pallas import tpu as pltpu
from jax.sharding import PartitionSpec as P

MESH = pl.DeviceIdType.MESH
STEPS = 10
ROWS = 16
COLS = 8
NB = 1024
SHARD = 64
LANES = 128
DIAG = STEPS * SHARD
PRIOR = 3712
PACKED = PRIOR // 2
HALF = PACKED // 2
SLAB = 512
SLABS = PRIOR // SLAB
TAIL = PRIOR - SLABS * SLAB
PARTS = ((0, DIAG // 2), (DIAG // 2, DIAG // 2), (DIAG, HALF), (DIAG + HALF, HALF))
STAGED = 1024
GROUPS = ((0, 1), (1, 2), (3, 7))


def split(value):
    high = value.astype(jnp.bfloat16)
    return high, (value - high.astype(jnp.float32)).astype(jnp.bfloat16)


def dot(left, right):
    return jnp.dot(left, right, preferred_element_type=jnp.float32)


def wrap(value, size=4):
    return lax.rem(value + size, size)


def kernel(
    target_ref, prior_ref, diag_ref, panel_ref, below_ref, out_ref,
    blocks, panel_high, panel_low, stage, factor, total, terms, arrived, held, own, weights, wide_high, wide_low,
    block_send, block_recv, stage_sem, factor_send, factor_recv, term_send, term_recv, send_sem, recv_sem,
):
    row = lax.axis_index("row")
    col = lax.axis_index("col")
    z, x = row // 4, lax.rem(row, 4)
    y, core = col // 2, lax.rem(col, 2)
    swap = core == 1
    first, second = jnp.where(swap, z, x), jnp.where(swap, x, z)
    chunk_of = lambda c: jnp.where(lax.rem(c, 2) == 1, 7 - c // 2, c // 2)
    mine = chunk_of(col)
    lane = lax.broadcasted_iota(jnp.int32, (1, LANES), 1)
    low_lanes = lane < 64

    def turn(value):
        return pltpu.roll(value, 64, 1)

    def panel_copy(q):
        width = min(STAGED, PRIOR - q * STAGED)
        return pltpu.make_async_copy(
            panel_ref.at[:, :, pl.ds(q * STAGED, width)], stage.at[q % 2, :, :, pl.ds(0, width)], stage_sem.at[q % 2, 0]
        )

    def below_copy(j, i):
        return pltpu.make_async_copy(
            below_ref.at[i * (i - 1) // 2 + j], stage.at[lax.rem(j, 2), i], stage_sem.at[lax.rem(j, 2), i]
        )

    panel_copy(0).start()
    panel_copy(1).start()

    barrier = pltpu.get_barrier_semaphore()
    for d in range(1, ROWS):
        pl.semaphore_signal(barrier, inc=1, device_id={"row": wrap(row + d, ROWS)}, device_id_type=MESH)
    for d in range(1, COLS):
        pl.semaphore_signal(barrier, inc=1, device_id={"col": wrap(col + d, COLS)}, device_id_type=MESH)

    lanes_of_mine = pl.ds(pl.multiple_of(mine * LANES, LANES), LANES)
    blocks[second, first, :DIAG] = diag_ref[:, :, lanes_of_mine].reshape(DIAG, LANES)
    for m in range(SLABS):
        piece = jnp.concatenate(
            [prior_ref[:, m * SLAB : m * SLAB + 256], prior_ref[:, m * SLAB + 256 : (m + 1) * SLAB]], axis=0
        )
        blocks[second, first, DIAG + 256 * m : DIAG + 256 * (m + 1)] = piece.T
    piece = prior_ref[:, SLABS * SLAB :].T
    blocks[second, first, DIAG + 256 * SLABS :] = jnp.concatenate([piece[:64], piece[64:]], axis=1)
    own[...] = target_ref[...]

    pl.semaphore_wait(barrier, ROWS + COLS - 2)

    def row_of(s, f):
        s, f = wrap(s), wrap(f)
        return jnp.where(swap, f * 4 + s, s * 4 + f)

    started = []

    def guarded(s, f, part, action):
        if part < 2:
            pl.when(row_of(s, f) >= 2 * mine)(action)
        else:
            action()

    def send(s_to, f_to, ds, df, part):
        s, f = wrap(s_to - ds), wrap(f_to - df)
        rows = pl.ds(*PARTS[part])
        copy = pltpu.make_async_remote_copy(
            src_ref=blocks.at[s, f, rows],
            dst_ref=blocks.at[s, f, rows],
            send_sem=block_send.at[len(started)],
            recv_sem=block_recv.at[wrap(ds), wrap(df), part],
            device_id={"row": row_of(s_to, f_to)},
            device_id_type=MESH,
        )
        guarded(s, f, part, copy.start)
        started.append((s, f, part, copy))

    def wait(ds, df, part):
        s, f = wrap(second - ds), wrap(first - df)
        rows = pl.ds(*PARTS[part])
        copy = pltpu.make_async_remote_copy(
            src_ref=blocks.at[s, f, rows],
            dst_ref=blocks.at[s, f, rows],
            send_sem=block_send.at[0],
            recv_sem=block_recv.at[ds, df, part],
            device_id={"row": row_of(second + 1, first)},
            device_id_type=MESH,
        )
        guarded(s, f, part, copy.wait_recv)

    def up(df, part):
        send(second + 1, first, 1, df, part)
        send(second - 1, first, 3, df, part)

    def begin(parts):
        for part in parts:
            send(second, first + 1, 0, 1, part)
            send(second, first - 1, 0, 3, part)
        for part in parts:
            up(0, part)

    def near(parts):
        for part in parts:
            wait(0, 1, part)
            if part % 2 == 0:
                send(second, first + 1, 0, 2, part)
            up(1, part)
            wait(0, 3, part)
            if part % 2 == 1:
                send(second, first - 1, 0, 2, part)
            up(3, part)

    def far(parts):
        for part in parts:
            wait(0, 2, part)
            up(2, part)

    def onward(df, parts):
        for part in parts:
            wait(1, df, part)
            wait(3, df, part)
            if part % 2 == 0:
                send(second + 1, first, 2, df, part)
            else:
                send(second - 1, first, 2, df, part)

    def last(df, parts):
        for part in parts:
            wait(2, df, part)

    begin((0, 1))
    begin((2, 3))

    for q in range(4):
        panel_copy(q).wait()
        width = min(STAGED, PRIOR - q * STAGED)
        for k in range(STEPS):
            high, low = split(stage[q % 2, k, :, :width])
            panel_high[k * SHARD : (k + 1) * SHARD, q * STAGED : q * STAGED + width] = high
            panel_low[k * SHARD : (k + 1) * SHARD, q * STAGED : q * STAGED + width] = low
        if q + 2 < 4:
            panel_copy(q + 2).start()

    def below_start(j):
        lax.fori_loop(j + 1, STEPS, lambda i, c: (below_copy(j, i).start(), c)[1], 0)

    below_start(0)
    below_start(1)

    near((0, 1))
    far((0, 1))
    near((2, 3))
    for df in (0, 1, 3, 2):
        onward(df, (0, 1))
    far((2, 3))
    for df in (0, 1, 3, 2):
        last(df, (0, 1))

    def times(block):
        high, low = split(block)
        both = dot(high, weights[...])
        return both[:, :LANES] + both[:, LANES:] + dot(low, weights[:, :LANES])

    def factor_step(j, carry):
        for r in range(ROWS):
            s, f = jnp.where(swap, r % 4, r // 4), jnp.where(swap, r // 4, r % 4)
            value = blocks[s, f, pl.ds(pl.multiple_of(j * SHARD, SHARD), SHARD)]
            high, low = split(jnp.where(r >= 2 * mine, value, 0.0))
            weights[r * SHARD : (r + 1) * SHARD, :LANES] = high
            weights[r * SHARD : (r + 1) * SHARD, LANES:] = low
        lax.fori_loop(j + 1, STEPS, lambda i, c: (below_copy(j, i).wait(), c)[1], 0)

        def three(g, carry):
            at = [jnp.minimum(j + 1 + 3 * g + t, STEPS - 1) for t in range(3)]
            result = times(jnp.concatenate([stage[lax.rem(j, 2), i] for i in at], axis=0))
            for t in range(3):
                factor[mine, at[t] * (at[t] - 1) // 2 + j] = result[t * SHARD : (t + 1) * SHARD]
            return carry

        lax.fori_loop(0, (STEPS - 1 - j + 2) // 3, three, 0)

        @pl.when(j + 2 < STEPS - 1)
        def _():
            below_start(j + 2)

        return carry

    lax.fori_loop(0, STEPS - 1, factor_step, 0)

    def factor_copy(k, source, to, half=None):
        part = factor.at[chunk_of(source)]
        if half is not None:
            part = part.at[pl.ds(half * 23, 23 - half)]
        return pltpu.make_async_remote_copy(
            src_ref=part,
            dst_ref=part,
            send_sem=factor_send.at[k],
            recv_sem=factor_recv.at[k],
            device_id={"col": to},
            device_id_type=MESH,
        )

    def side(dy, other=0):
        return wrap(y + dy) * 2 + (1 - core if other else core)

    factor_copy(1, col, side(1)).start()
    factor_copy(2, col, side(-1)).start()
    factor_copy(0, col, side(0, 1)).start()

    def slab_weights(rows_of, height):
        parts = [rows_of(f) for f in range(4)]
        turned = [turn(p) for p in parts]
        upper = [jnp.where(low_lanes, parts[f], turned[f + 1]) for f in (0, 2)]
        lower = [jnp.where(low_lanes, turned[f], parts[f + 1]) for f in (0, 2)]
        for side_at, values in ((0, upper), (height, lower)):
            for n in range(2):
                high, low = split(values[n])
                wide_high[side_at : side_at + height, n * LANES : (n + 1) * LANES] = high
                wide_low[side_at : side_at + height, n * LANES : (n + 1) * LANES] = low

    def panel_term(columns, depth):
        high = panel_high[:, columns]
        return (
            dot(high, wide_high[:depth])
            + dot(high, wide_low[:depth])
            + dot(panel_low[:, columns], wide_high[:depth])
        )

    def panel_product(s):
        def slab(m, carry):
            at = pl.multiple_of(DIAG + 256 * m, 256 if DIAG % 256 == 0 else 128)
            slab_weights(lambda f: blocks[s, f, pl.ds(at, 256)], 256)
            total[...] += panel_term(pl.ds(pl.multiple_of(m * SLAB, SLAB), SLAB), SLAB)
            return carry

        slab_weights(lambda f: blocks[s, f, DIAG + 256 * SLABS :], 64)
        total[...] = panel_term(pl.ds(SLABS * SLAB, TAIL), TAIL)
        lax.fori_loop(0, SLABS, slab, 0)

        @pl.when(core == 0)
        def _():
            for n in range(2):
                terms[2 * s + n] = total[:, n * LANES : (n + 1) * LANES].reshape(STEPS, SHARD, LANES)

        @pl.when(core == 1)
        def _():
            odd = lax.rem(s, 2)
            keep = lane // 64 == odd
            for f in range(4):
                value = total[:, (f // 2) * LANES : (f // 2 + 1) * LANES]
                value = jnp.where(odd == f % 2, value, turn(value)).reshape(STEPS, SHARD, LANES)
                at = 2 * f + s // 2
                terms[at] = jnp.where(keep.reshape(1, 1, LANES), value, terms[at])

    def term_copy(source, to, g):
        steps = pl.ds(*GROUPS[g])
        return pltpu.make_async_remote_copy(
            src_ref=terms.at[to, steps],
            dst_ref=arrived.at[source, steps],
            send_sem=term_send.at[to, g],
            recv_sem=term_recv.at[source, g],
            device_id={"col": to},
            device_id_type=MESH,
        )

    def give(targets):
        for g in range(len(GROUPS)):
            for to in targets:
                pl.when(to != col)(lambda to=to, g=g: term_copy(col, to, g).start())

    def give_zero(s):
        pl.when(core == 0)(lambda: give([2 * s, 2 * s + 1]))

    def give_one(half):
        pl.when(core == 1)(lambda: give([2 * f + half for f in range(4)]))

    panel_product(second)
    give_zero(second)
    for df in (0, 1, 3, 2):
        onward(df, (2, 3))

    factor_copy(1, side(-1), side(1)).wait_recv()
    factor_copy(3, side(-1), side(1), 0).start()
    factor_copy(5, side(-1), side(0, 1)).start()
    factor_copy(2, side(1), side(-1)).wait_recv()
    factor_copy(4, side(1), side(-1), 1).start()
    factor_copy(6, side(1), side(0, 1)).start()

    even = lax.rem(second, 2) == 0
    pair = jnp.where(even, second + 1, second - 1)
    other = wrap(pair + 2)
    panel_product(pair)
    give_zero(pair)
    give_one(second // 2)
    panel_product(other)
    give_zero(other)

    factor_copy(3, side(2), side(1), 0).wait_recv()
    factor_copy(4, side(2), side(1), 1).wait_recv()
    factor_copy(7, side(2), side(0, 1)).start()

    for df in (0, 1, 3, 2):
        last(df, (2, 3))
    panel_product(wrap(second + 2))
    give_zero(wrap(second + 2))
    give_one(1 - second // 2)

    factor_copy(0, side(0, 1), col).wait_recv()
    factor_copy(5, side(-1, 1), col).wait_recv()
    factor_copy(6, side(1, 1), col).wait_recv()
    factor_copy(7, side(2, 1), col).wait_recv()

    def ready(g):
        begin_at, count = GROUPS[g]
        for d in range(1, COLS):
            term_copy(wrap(col + d, COLS), col, g).wait_recv()
        for k in range(begin_at, begin_at + count):
            value = terms[col, k]
            for d in range(1, COLS):
                value = value + arrived[wrap(col + d, COLS), k]
            own[k] -= value

    def copy(k, d):
        slot = lax.rem(k, 2)
        return pltpu.make_async_remote_copy(
            src_ref=own.at[k],
            dst_ref=held.at[slot, row],
            send_sem=send_sem.at[slot, d],
            recv_sem=recv_sem.at[slot, d],
            device_id={"row": wrap(row + d, ROWS)},
            device_id_type=MESH,
        )

    def spread(k):
        for d in range(1, ROWS):
            copy(k, d).start()
        held[lax.rem(k, 2), row] = own[k]

    def arrive(k):
        for d in range(1, ROWS):
            copy(k, d).wait_recv()
        high, low = split(held[lax.rem(k, 2)].reshape(NB, LANES))
        weights[...] = jnp.concatenate([high, low], axis=1)

    def coupling(i, k):
        at = i * (i - 1) // 2 + k
        return jnp.concatenate([factor[c, at] for c in range(COLS)], axis=1)

    ready(0)
    spread(0)

    def step(k, carry):
        @pl.when(k == 0)
        def _():
            ready(1)

        @pl.when(k == 2)
        def _():
            ready(2)

        arrive(k)
        own[k + 1] -= times(coupling(k + 1, k))
        spread(k + 1)
        out_ref[k] = times(diag_ref[k])

        def later(i, carry):
            own[i] -= times(coupling(i, k))
            return carry

        lax.fori_loop(k + 2, STEPS, later, 0)
        for d in range(1, ROWS):
            copy(k, d).wait_send()
        return carry

    lax.fori_loop(0, STEPS - 1, step, 0)
    arrive(STEPS - 1)
    out_ref[STEPS - 1] = times(diag_ref[STEPS - 1])

    for d in range(1, ROWS):
        copy(STEPS - 1, d).wait_send()
    for s, f, part, sent in started:
        guarded(s, f, part, sent.wait_send)
    for k, half in enumerate((None, None, None, 0, 1, None, None, None)):
        factor_copy(k, col, side(1), half).wait_send()
    for g in range(len(GROUPS)):
        for d in range(1, COLS):
            term_copy(col, wrap(col + d, COLS), g).wait_send()


def on_device(targets, lower_panel, prior_solution, diag_inverse, below_blocks):
    f32, bf16 = jnp.float32, jnp.bfloat16
    vmem = pl.BlockSpec(memory_space=pltpu.VMEM)
    hbm = pl.BlockSpec(memory_space=pl.ANY)
    dma = pltpu.SemaphoreType.DMA
    return pl.pallas_call(
        kernel,
        out_shape=jax.ShapeDtypeStruct(targets.shape, f32),
        in_specs=[vmem, vmem, vmem, hbm, hbm],
        out_specs=vmem,
        scratch_shapes=[
            pltpu.VMEM((4, 4, DIAG + PACKED, LANES), f32),
            pltpu.VMEM((DIAG, PRIOR), bf16),
            pltpu.VMEM((DIAG, PRIOR), bf16),
            pltpu.VMEM((2, STEPS, SHARD, STAGED), f32),
            pltpu.VMEM((COLS, STEPS * (STEPS - 1) // 2, SHARD, LANES), f32),
            pltpu.VMEM((DIAG, 2 * LANES), f32),
            pltpu.VMEM((COLS, STEPS, SHARD, LANES), f32),
            pltpu.VMEM((COLS, STEPS, SHARD, LANES), f32),
            pltpu.VMEM((2, ROWS, SHARD, LANES), f32),
            pltpu.VMEM((STEPS, SHARD, LANES), f32),
            pltpu.VMEM((NB, 2 * LANES), bf16),
            pltpu.VMEM((SLAB, 2 * LANES), bf16),
            pltpu.VMEM((SLAB, 2 * LANES), bf16),
            dma((64,)),
            dma((4, 4, 4)),
            dma((2, STEPS)),
            dma((8,)),
            dma((8,)),
            dma((COLS, len(GROUPS))),
            dma((COLS, len(GROUPS))),
            dma((2, ROWS)),
            dma((2, ROWS)),
        ],
        compiler_params=pltpu.CompilerParams(collective_id=0, has_side_effects=True, vmem_limit_bytes=63 << 20),
    )(targets, prior_solution.T, diag_inverse, lower_panel, below_blocks)


def solution(mesh):
    in_specs = (
        P(None, "row", "col"),
        P(None, "row", "col"),
        P("col", "row"),
        P(None, "row", None),
        P(None, "row", None),
    )
    out_specs = P(None, "row", "col")
    return jax.shard_map(
        on_device, mesh=mesh, in_specs=in_specs, out_specs=out_specs, check_vma=False
    )
```

time: 422 us -> 256 us (0.61)
  waiting for transfers between devices: 178 us -> 0 us
  Pallas kernels: 92.4 us -> 253 us
  matrix products: 131 us -> 0 us
  between operations: 13.2 us -> 0.01 us
    all_gather x3 -> x0, waiting for transfers between devices: 178 us -> none  [the longest x1 60.9 us: on_device(): coupling = lax.all_gather(jnp.stack(parts), 'col', axis=0)]
    pallas_call x1, Pallas kernels: 92.4 us -> 253 us  [on_device(): pl.pallas_call(kernel, out_shape=jax.ShapeDtypeStruct(targets.shape, f32)...]
    dot_general x46 -> x0, matrix products: 131 us -> none  [product(): jnp.dot(left, right, precision=lax.Precision.HIGHEST, preferred_element_t...]
  transfers between devices with their start and end apart: 4 -> 0, of which waited for: 3 -> 0; matrix products, arithmetic and copies ran while one was open for 23% -> 0% of each run, Pallas kernels for 0% -> 0%
where the time goes in v2:
time: 256 us; the launch traced here: 255 us
  Pallas kernels  253 us (99%)
    pallas_call x1, Pallas kernels, on_device(): pl.pallas_call(kernel, out_shape=jax.ShapeDtypeStruct(targets.shape, f32)...  253 us

profile of v2, /device:TPU:24, one launch (start us, length us, event | category | flops | bytes accessed | tf_op | source)
XLA Modules:
  0.0 254.8 jit_solution(720570455039891750)
XLA Ops:
  0.0 253.0 %shard_map.55 = f32[10,64,128]{2,1,0:T(8,128)} custom-call(f32[10,64,128]{2,1,0:T(8,128)} %target_ref.1, f32[64,3712]{1,0:T(8,128)} %bitcast.1, f32[10,64,1024]{2,1,0:T(8,128)} %diag_ref.1, f32[10,64,3712]{2,1,0:T(8,128)} %panel_ref.1, f32[45,64,1024]{2,1,0:T(8,128)} %below_ref.1), custom_call_target="tpu_custom_call" | custom-call | tf_op jit(solution)/shard_map/pallas_call | solution.py:435
  253.1 1.7 copy.7

commit v3 on v2

v3 whole, which is shorter than its diff:
```python
import jax
import jax.numpy as jnp
from jax import lax
from jax.experimental import pallas as pl
from jax.experimental.pallas import tpu as pltpu
from jax.sharding import PartitionSpec as P

MESH = pl.DeviceIdType.MESH
STEPS = 10
ROWS = 16
COLS = 8
NB = 1024
SHARD = 64
LANES = 128
DIAG = STEPS * SHARD
PRIOR = 3712
PACKED = PRIOR // 2
SLAB = 512
SLABS = PRIOR // SLAB
TAIL = PRIOR - SLABS * SLAB
TAKEN = (STEPS // 2) * SHARD
EARLY = 1024
LATE = PACKED - EARLY
PARTS = tuple((n * TAKEN // 2, TAKEN // 2) for n in range(4)) + (
    (DIAG, EARLY // 2),
    (DIAG + EARLY // 2, EARLY // 2),
    (DIAG + EARLY, LATE // 2),
    (DIAG + EARLY + LATE // 2, LATE // 2),
)
SMALL, FRONT, BACK = (0, 1, 2, 3), (4, 5), (6, 7)
ORDER = (0, 1, 3, 2)
PEERS = (10, 6, 14, 9, 11, 5, 15, 7, 13, 8, 2, 4, 1, 12, 3)
PAIRS = STEPS * (STEPS - 1) // 2
STAGED = 1024
GROUPS = ((0, 1), (1, 2), (3, 7))


def split(value):
    high = value.astype(jnp.bfloat16)
    return high, (value - high.astype(jnp.float32)).astype(jnp.bfloat16)


def dot(left, right):
    return jnp.dot(left, right, preferred_element_type=jnp.float32)


def pairs_of(j):
    return (STEPS - 1) * j - j * (j - 1) // 2, STEPS - 1 - j


def wrap(value, size=4):
    return lax.rem(value + size, size)


def kernel(
    target_ref, prior_ref, diag_ref, panel_ref, below_ref, out_ref,
    blocks, panel_high, panel_low, stage, factor, total, terms, arrived, held, own, weights, wide_high, wide_low,
    block_send, block_recv, stage_sem, factor_send, factor_recv, term_send, term_recv, send_sem, recv_sem,
):
    row = lax.axis_index("row")
    col = lax.axis_index("col")
    z, x = row // 4, lax.rem(row, 4)
    y, core = col // 2, lax.rem(col, 2)
    swap = core == 1
    second = jnp.where(swap, x, z)
    groups = (y, 7 - y)
    lane = lax.broadcasted_iota(jnp.int32, (1, LANES), 1)
    low_lanes = lane < 64

    def turn(value):
        return pltpu.roll(value, 64, 1)

    def panel_copy(q):
        width = min(STAGED, PRIOR - q * STAGED)
        return pltpu.make_async_copy(
            panel_ref.at[:, :, pl.ds(q * STAGED, width)], stage.at[q % 2, :, :, pl.ds(0, width)], stage_sem.at[q % 2, 0]
        )

    def below_copy(j, i):
        slot = j // 2 % 2
        return pltpu.make_async_copy(below_ref.at[i * (i - 1) // 2 + j], stage.at[slot, i], stage_sem.at[slot, i])

    panel_copy(0).start()
    panel_copy(1).start()

    barrier = pltpu.get_barrier_semaphore()
    for d in range(1, ROWS):
        pl.semaphore_signal(barrier, inc=1, device_id={"row": wrap(row + d, ROWS)}, device_id_type=MESH)
    for d in range(1, COLS):
        pl.semaphore_signal(barrier, inc=1, device_id={"col": wrap(col + d, COLS)}, device_id_type=MESH)

    for n in range(2):
        lanes = pl.ds(pl.multiple_of(groups[n] * LANES, LANES), LANES)
        for t in range(STEPS // 2):
            blocks[row, n * TAKEN + t * SHARD : n * TAKEN + (t + 1) * SHARD] = diag_ref[2 * t + core, :, lanes]
    for m in range(SLABS):
        piece = jnp.concatenate(
            [prior_ref[:, m * SLAB : m * SLAB + 256], prior_ref[:, m * SLAB + 256 : (m + 1) * SLAB]], axis=0
        )
        blocks[row, DIAG + 256 * m : DIAG + 256 * (m + 1)] = piece.T
    piece = prior_ref[:, SLABS * SLAB :].T
    blocks[row, DIAG + 256 * SLABS :] = jnp.concatenate([piece[:64], piece[64:]], axis=1)
    own[...] = target_ref[...]

    pl.semaphore_wait(barrier, ROWS + COLS - 2)

    def turned_of(part):
        return jnp.bool_(True) if part in (2, 3) else swap

    def place(part):
        turned = turned_of(part)
        return jnp.where(turned, x, z), jnp.where(turned, z, x)

    def row_of(part, s, f):
        s, f = wrap(s), wrap(f)
        return jnp.where(turned_of(part), f * 4 + s, s * 4 + f)

    started = []

    def guarded(source, part, action):
        if part in SMALL:
            pl.when(source >= 2 * groups[part // 2])(action)
        else:
            action()

    def send(part, to_s, to_f, ds, df):
        s, f = place(part)
        source = row_of(part, s + to_s - ds, f + to_f - df)
        piece = blocks.at[source, pl.ds(*PARTS[part])]
        copy = pltpu.make_async_remote_copy(
            src_ref=piece,
            dst_ref=piece,
            send_sem=block_send.at[len(started)],
            recv_sem=block_recv.at[ds, df, part],
            device_id={"row": row_of(part, s + to_s, f + to_f)},
            device_id_type=MESH,
        )
        guarded(source, part, copy.start)
        started.append((source, part, copy))

    def wait(part, ds, df):
        s, f = place(part)
        source = row_of(part, s - ds, f - df)
        piece = blocks.at[source, pl.ds(*PARTS[part])]
        copy = pltpu.make_async_remote_copy(
            src_ref=piece,
            dst_ref=piece,
            send_sem=block_send.at[0],
            recv_sem=block_recv.at[ds, df, part],
            device_id={"row": row_of(part, s + 1, f)},
            device_id_type=MESH,
        )
        guarded(source, part, copy.wait_recv)

    def up(df, part):
        send(part, 1, 0, 1, df)
        send(part, -1, 0, 3, df)

    def begin(parts):
        for part in parts:
            send(part, 0, 1, 0, 1)
            send(part, 0, -1, 0, 3)
            up(0, part)

    def near(parts):
        for part in parts:
            wait(part, 0, 1)
            if part % 2 == 0:
                send(part, 0, 1, 0, 2)
            up(1, part)
            wait(part, 0, 3)
            if part % 2 == 1:
                send(part, 0, -1, 0, 2)
            up(3, part)

    def far(parts):
        for part in parts:
            wait(part, 0, 2)
            up(2, part)

    def onward(df, parts):
        for part in parts:
            wait(part, 1, df)
            wait(part, 3, df)
            if part % 2 == 0:
                send(part, 1, 0, 2, df)
            else:
                send(part, -1, 0, 2, df)

    def last(df, parts):
        for part in parts:
            wait(part, 2, df)

    begin(SMALL)

    def convert(q):
        panel_copy(q).wait()
        width = min(STAGED, PRIOR - q * STAGED)
        for k in range(STEPS):
            high, low = split(stage[q % 2, k, :, :width])
            panel_high[k * SHARD : (k + 1) * SHARD, q * STAGED : q * STAGED + width] = high
            panel_low[k * SHARD : (k + 1) * SHARD, q * STAGED : q * STAGED + width] = low
        if q + 2 < 4:
            panel_copy(q + 2).start()

    convert(0)
    convert(1)
    near(SMALL)
    far(SMALL)
    begin(FRONT)
    begin(BACK)
    convert(2)
    convert(3)

    def below_start(j):
        for i in range(j + 1, STEPS):
            below_copy(j, i).start()

    def on_own(j, action):
        if j < STEPS - 1:
            pl.when(core == j % 2)(lambda: action(j))

    for j in range(4):
        on_own(j, below_start)

    for df in ORDER:
        onward(df, SMALL)
    near(FRONT)
    for df in ORDER:
        last(df, SMALL)
    near(BACK)

    def factor_copy(j, way, source, to):
        at, count = pairs_of(j)
        part = factor.at[source, pl.ds(at, count)]
        return pltpu.make_async_remote_copy(
            src_ref=part,
            dst_ref=part,
            send_sem=factor_send.at[j, way],
            recv_sem=factor_recv.at[j, way],
            device_id={"col": to},
            device_id_type=MESH,
        )

    def at_y(dy):
        return wrap(y + dy)

    same = lambda dy: at_y(dy) * 2 + core
    partner = y * 2 + 1 - core

    def make_factor(j):
        t = j // 2
        for n in range(2):
            for r in range(ROWS):
                value = blocks[r, n * TAKEN + t * SHARD : n * TAKEN + (t + 1) * SHARD]
                high, low = split(jnp.where(r >= 2 * groups[n], value, 0.0))
                wide_high[r * SHARD : (r + 1) * SHARD, n * LANES : (n + 1) * LANES] = high
                wide_low[r * SHARD : (r + 1) * SHARD, n * LANES : (n + 1) * LANES] = low
        at, count = pairs_of(j)
        for i in range(j + 1, STEPS):
            below_copy(j, i).wait()
        for begin_at in range(0, count, 3):
            n = min(3, count - begin_at)
            i = j + 1 + begin_at
            high, low = split(stage[t % 2, i : i + n].reshape(n * SHARD, NB))
            result = dot(high, wide_high[...]) + dot(high, wide_low[...]) + dot(low, wide_high[...])
            factor[y, at + begin_at : at + begin_at + n] = result.reshape(n, SHARD, 2 * LANES)
        if j + 4 < STEPS - 1:
            below_start(j + 4)
        factor_copy(j, 1, y, same(1)).start()
        factor_copy(j, 2, y, same(-1)).start()
        factor_copy(j, 0, y, partner).start()

    for j in range(STEPS - 1):
        on_own(j, make_factor)

    def up_goes(j):
        return j // 2 % 2 == 0

    def hop(j):
        way, dy = (1, -1) if up_goes(j) else (2, 1)
        factor_copy(j, way, at_y(dy), same(-dy)).wait_recv()
        factor_copy(j, 3, at_y(dy), same(-dy)).start()
        factor_copy(j, 3 + way, at_y(dy), partner).start()

    def pass_on(j):
        way, dy = (2, 1) if up_goes(j) else (1, -1)
        factor_copy(j, way, at_y(dy), same(1)).wait_recv()
        factor_copy(j, 3 + way, at_y(dy), partner).start()
        factor_copy(j, 3, at_y(2), same(1)).wait_recv()
        factor_copy(j, 6, at_y(2), partner).start()

    def need(j):
        @pl.when(core != j % 2)
        def _():
            for way, dy in ((0, 0), (4, -1), (5, 1), (6, 2)):
                factor_copy(j, way, at_y(dy), partner).wait_recv()

    def slab_weights(rows_of, height):
        parts = [rows_of(f) for f in range(4)]
        turned = [turn(p) for p in parts]
        upper = [jnp.where(low_lanes, parts[f], turned[f + 1]) for f in (0, 2)]
        lower = [jnp.where(low_lanes, turned[f], parts[f + 1]) for f in (0, 2)]
        for side_at, values in ((0, upper), (height, lower)):
            for n in range(2):
                high, low = split(values[n])
                wide_high[side_at : side_at + height, n * LANES : (n + 1) * LANES] = high
                wide_low[side_at : side_at + height, n * LANES : (n + 1) * LANES] = low

    def panel_term(columns, depth):
        high = panel_high[:, columns]
        return (
            dot(high, wide_high[:depth])
            + dot(high, wide_low[:depth])
            + dot(panel_low[:, columns], wide_high[:depth])
        )

    def group_row(s, f):
        return jnp.where(swap, f * 4 + s, s * 4 + f)

    def panel_half(s, back):
        def slab(m, carry):
            at = pl.multiple_of(DIAG + 256 * m, LANES)
            slab_weights(lambda f: blocks[group_row(s, f), pl.ds(at, 256)], 256)
            total[...] += panel_term(pl.ds(pl.multiple_of(m * SLAB, SLAB), SLAB), SLAB)
            return carry

        if back:
            slab_weights(lambda f: blocks[group_row(s, f), DIAG + 256 * SLABS :], 64)
            total[...] += panel_term(pl.ds(SLABS * SLAB, TAIL), TAIL)
            lax.fori_loop(EARLY // 256, SLABS, slab, 0)
        else:
            total[...] = jnp.zeros_like(total)
            lax.fori_loop(0, EARLY // 256, slab, 0)

    def keep_terms(s):
        @pl.when(core == 0)
        def _():
            for n in range(2):
                terms[2 * s + n] = total[:, n * LANES : (n + 1) * LANES].reshape(STEPS, SHARD, LANES)

        @pl.when(core == 1)
        def _():
            odd = lax.rem(s, 2)
            keep = lane // 64 == odd
            for f in range(4):
                value = total[:, (f // 2) * LANES : (f // 2 + 1) * LANES]
                value = jnp.where(odd == f % 2, value, turn(value)).reshape(STEPS, SHARD, LANES)
                at = 2 * f + s // 2
                terms[at] = jnp.where(keep.reshape(1, 1, LANES), value, terms[at])

    def panel_product(s):
        panel_half(s, False)
        panel_half(s, True)
        keep_terms(s)

    def term_copy(source, to, g):
        steps = pl.ds(*GROUPS[g])
        return pltpu.make_async_remote_copy(
            src_ref=terms.at[to, steps],
            dst_ref=arrived.at[source, steps],
            send_sem=term_send.at[to, g],
            recv_sem=term_recv.at[source, g],
            device_id={"col": to},
            device_id_type=MESH,
        )

    def give(targets):
        for g in range(len(GROUPS)):
            for to in targets:
                pl.when(to != col)(lambda to=to, g=g: term_copy(col, to, g).start())

    def give_zero(s):
        pl.when(core == 0)(lambda: give([2 * s, 2 * s + 1]))

    def give_one(half):
        pl.when(core == 1)(lambda: give([2 * f + half for f in range(4)]))

    far(FRONT)
    far(BACK)
    panel_product(second)
    give_zero(second)
    for df, parts in ((0, FRONT), (1, FRONT), (3, FRONT), (0, BACK), (1, BACK), (3, BACK), (2, FRONT), (2, BACK)):
        onward(df, parts)

    even = lax.rem(second, 2) == 0
    pair = jnp.where(even, second + 1, second - 1)
    other = wrap(pair + 2)
    panel_product(pair)
    give_zero(pair)
    give_one(second // 2)
    for j in range(2):
        on_own(j, hop)
    panel_product(other)
    give_zero(other)
    for j in range(2, STEPS - 1):
        on_own(j, hop)
    for df in ORDER:
        last(df, FRONT)
    panel_half(wrap(second + 2), False)
    for j in range(2):
        on_own(j, pass_on)
    for df in ORDER:
        last(df, BACK)
    panel_half(wrap(second + 2), True)
    keep_terms(wrap(second + 2))
    give_zero(wrap(second + 2))
    give_one(1 - second // 2)

    def ready(g):
        begin_at, count = GROUPS[g]
        for d in range(1, COLS):
            term_copy(wrap(col + d, COLS), col, g).wait_recv()
        for k in range(begin_at, begin_at + count):
            value = terms[col, k]
            for d in range(1, COLS):
                value = value + arrived[wrap(col + d, COLS), k]
            own[k] -= value

    def copy(k, d):
        slot = k % 2
        return pltpu.make_async_remote_copy(
            src_ref=own.at[k],
            dst_ref=held.at[slot, row],
            send_sem=send_sem.at[slot, d],
            recv_sem=recv_sem.at[slot, d],
            device_id={"row": wrap(row + d, ROWS)},
            device_id_type=MESH,
        )

    def spread(k):
        for d in PEERS:
            copy(k, d).start()
        held[k % 2, row] = own[k]

    def arrive(k):
        for d in range(1, ROWS):
            copy(k, d).wait_recv()
        high, low = split(held[k % 2].reshape(NB, LANES))
        weights[...] = jnp.concatenate([high, low], axis=1)

    def times(block):
        high, low = split(block)
        both = dot(high, weights[...])
        return both[:, :LANES] + both[:, LANES:] + dot(low, weights[:, :LANES])

    def coupling(k, begin_at, end_at):
        at, _ = pairs_of(k)
        rows = slice(at + begin_at, at + end_at)
        parts = [factor[c, rows, :, :LANES] for c in range(4)] + [factor[c, rows, :, LANES:] for c in (3, 2, 1, 0)]
        return jnp.concatenate([p.reshape(-1, LANES) for p in parts], axis=1)

    ready(0)
    spread(0)
    for k in range(STEPS - 1):
        if k == 0:
            ready(1)
        if k == 2:
            ready(2)
        need(k)
        arrive(k)
        own[k + 1] -= times(coupling(k, 0, 1))
        spread(k + 1)
        if k + 2 < STEPS - 1:
            on_own(k + 2, pass_on)
        out_ref[k] = times(diag_ref[k])
        for i in range(k + 2, STEPS, 3):
            end_at = min(i + 3, STEPS)
            result = times(coupling(k, i - k - 1, end_at - k - 1))
            own[i:end_at] -= result.reshape(end_at - i, SHARD, LANES)
        for d in range(1, ROWS):
            copy(k, d).wait_send()
    arrive(STEPS - 1)
    out_ref[STEPS - 1] = times(diag_ref[STEPS - 1])

    for d in range(1, ROWS):
        copy(STEPS - 1, d).wait_send()
    for source, part, sent in started:
        guarded(source, part, sent.wait_send)
    for j in range(STEPS - 1):
        on_own(j, lambda j: [factor_copy(j, way, y, partner).wait_send() for way in range(7)] and None)
    for g in range(len(GROUPS)):
        for d in range(1, COLS):
            term_copy(col, wrap(col + d, COLS), g).wait_send()


def on_device(targets, lower_panel, prior_solution, diag_inverse, below_blocks):
    f32, bf16 = jnp.float32, jnp.bfloat16
    vmem = pl.BlockSpec(memory_space=pltpu.VMEM)
    hbm = pl.BlockSpec(memory_space=pl.ANY)
    dma = pltpu.SemaphoreType.DMA
    return pl.pallas_call(
        kernel,
        out_shape=jax.ShapeDtypeStruct(targets.shape, f32),
        in_specs=[vmem, vmem, vmem, hbm, hbm],
        out_specs=vmem,
        scratch_shapes=[
            pltpu.VMEM((ROWS, DIAG + PACKED, LANES), f32),
            pltpu.VMEM((DIAG, PRIOR), bf16),
            pltpu.VMEM((DIAG, PRIOR), bf16),
            pltpu.VMEM((2, STEPS, SHARD, STAGED), f32),
            pltpu.VMEM((4, PAIRS, SHARD, 2 * LANES), f32),
            pltpu.VMEM((DIAG, 2 * LANES), f32),
            pltpu.VMEM((COLS, STEPS, SHARD, LANES), f32),
            pltpu.VMEM((COLS, STEPS, SHARD, LANES), f32),
            pltpu.VMEM((2, ROWS, SHARD, LANES), f32),
            pltpu.VMEM((STEPS, SHARD, LANES), f32),
            pltpu.VMEM((NB, 2 * LANES), bf16),
            pltpu.VMEM((NB, 2 * LANES), bf16),
            pltpu.VMEM((NB, 2 * LANES), bf16),
            dma((15 * len(PARTS),)),
            dma((4, 4, len(PARTS))),
            dma((2, STEPS)),
            dma((STEPS - 1, 7)),
            dma((STEPS - 1, 7)),
            dma((COLS, len(GROUPS))),
            dma((COLS, len(GROUPS))),
            dma((2, ROWS)),
            dma((2, ROWS)),
        ],
        compiler_params=pltpu.CompilerParams(collective_id=0, has_side_effects=True, vmem_limit_bytes=63 << 20),
    )(targets, prior_solution.T, diag_inverse, lower_panel, below_blocks)


def solution(mesh):
    in_specs = (
        P(None, "row", "col"),
        P(None, "row", "col"),
        P("col", "row"),
        P(None, "row", None),
        P(None, "row", None),
    )
    out_specs = P(None, "row", "col")
    return jax.shard_map(
        on_device, mesh=mesh, in_specs=in_specs, out_specs=out_specs, check_vma=False
    )
```

time: 256 us -> 225 us (0.88)
  Pallas kernels: 253 us -> 223 us
    pallas_call x1, Pallas kernels: 253 us -> 223 us  [on_device(): pl.pallas_call(kernel, out_shape=jax.ShapeDtypeStruct(targets.shape, f32)...]
where the time goes in v3:
time: 225 us; the launch traced here: 224 us
  Pallas kernels  223 us (99%)
    pallas_call x1, Pallas kernels, on_device(): pl.pallas_call(kernel, out_shape=jax.ShapeDtypeStruct(targets.shape, f32)...  223 us

profile of v3, /device:TPU:24, one launch (start us, length us, event | category | flops | bytes accessed | tf_op | source)
XLA Modules:
  0.0 224.5 jit_solution(16653368442078751604)
XLA Ops:
  0.0 222.8 %shard_map.55 = f32[10,64,128]{2,1,0:T(8,128)} custom-call(f32[10,64,128]{2,1,0:T(8,128)} %target_ref.1, f32[64,3712]{1,0:T(8,128)} %bitcast.1, f32[10,64,1024]{2,1,0:T(8,128)} %diag_ref.1, f32[10,64,3712]{2,1,0:T(8,128)} %panel_ref.1, f32[45,64,1024]{2,1,0:T(8,128)} %below_ref.1), custom_call_target="tpu_custom_call" | custom-call | tf_op jit(solution)/shard_map/pallas_call | solution.py:492
  222.8 1.7 copy.7

commit v4 on v3

--- a/solution.py
+++ b/solution.py
@@ -21,18 +21,25 @@
 TAKEN = (STEPS // 2) * SHARD
 EARLY = 1024
 LATE = PACKED - EARLY
-PARTS = tuple((n * TAKEN // 2, TAKEN // 2) for n in range(4)) + (
+PARTS = (
+    (0, 128),
+    (128, 128),
+    (256, 64),
+    (TAKEN, 128),
+    (TAKEN + 128, 128),
+    (TAKEN + 256, 64),
     (DIAG, EARLY // 2),
     (DIAG + EARLY // 2, EARLY // 2),
     (DIAG + EARLY, LATE // 2),
     (DIAG + EARLY + LATE // 2, LATE // 2),
 )
-SMALL, FRONT, BACK = (0, 1, 2, 3), (4, 5), (6, 7)
+SMALL, FRONT, BACK = (0, 1, 2, 3, 4, 5), (6, 7), (8, 9)
 ORDER = (0, 1, 3, 2)
 PEERS = (10, 6, 14, 9, 11, 5, 15, 7, 13, 8, 2, 4, 1, 12, 3)
 PAIRS = STEPS * (STEPS - 1) // 2
 STAGED = 1024
-GROUPS = ((0, 1), (1, 2), (3, 7))
+GROUPS = ((0, 1), (1, 2), (3, 3), (6, 4))
+AHEAD = 4
 
 
 def split(value):
@@ -105,7 +112,7 @@
     pl.semaphore_wait(barrier, ROWS + COLS - 2)
 
     def turned_of(part):
-        return jnp.bool_(True) if part in (2, 3) else swap
+        return jnp.bool_(True) if part in (3, 4, 5) else swap
 
     def place(part):
         turned = turned_of(part)
@@ -119,7 +126,8 @@
 
     def guarded(source, part, action):
         if part in SMALL:
-            pl.when(source >= 2 * groups[part // 2])(action)
+            needed = source >= 2 * groups[part // 3]
+            pl.when(jnp.logical_and(needed, core == 0) if part in (2, 5) else needed)(action)
         else:
             action()
 
@@ -228,7 +236,6 @@
     near(FRONT)
     for df in ORDER:
         last(df, SMALL)
-    near(BACK)
 
     def factor_copy(j, way, source, to):
         at, count = pairs_of(j)
@@ -247,6 +254,11 @@
 
     same = lambda dy: at_y(dy) * 2 + core
     partner = y * 2 + 1 - core
+
+    def share(j):
+        factor_copy(j, 1, y, same(1)).start()
+        factor_copy(j, 2, y, same(-1)).start()
+        factor_copy(j, 0, y, partner).start()
 
     def make_factor(j):
         t = j // 2
@@ -267,12 +279,12 @@
             factor[y, at + begin_at : at + begin_at + n] = result.reshape(n, SHARD, 2 * LANES)
         if j + 4 < STEPS - 1:
             below_start(j + 4)
-        factor_copy(j, 1, y, same(1)).start()
-        factor_copy(j, 2, y, same(-1)).start()
-        factor_copy(j, 0, y, partner).start()
+        if j < AHEAD:
+            share(j)
 
     for j in range(STEPS - 1):
         on_own(j, make_factor)
+    near(BACK)
 
     def up_goes(j):
         return j // 2 % 2 == 0
@@ -366,7 +378,7 @@
         )
 
     def give(targets):
-        for g in range(len(GROUPS)):
+        for g in range(len(GROUPS) - 1):
             for to in targets:
                 pl.when(to != col)(lambda to=to, g=g: term_copy(col, to, g).start())
 
@@ -393,7 +405,7 @@
         on_own(j, hop)
     panel_product(other)
     give_zero(other)
-    for j in range(2, STEPS - 1):
+    for j in range(2, AHEAD):
         on_own(j, hop)
     for df in ORDER:
         last(df, FRONT)
@@ -457,12 +469,23 @@
             ready(1)
         if k == 2:
             ready(2)
+        if k == 5:
+            ready(3)
         need(k)
         arrive(k)
         own[k + 1] -= times(coupling(k, 0, 1))
         spread(k + 1)
-        if k + 2 < STEPS - 1:
+        if k + 2 < AHEAD:
             on_own(k + 2, pass_on)
+        if k == 0:
+            for d in range(1, COLS):
+                term_copy(col, wrap(col + d, COLS), len(GROUPS) - 1).start()
+        if AHEAD <= k + 4 < STEPS - 1:
+            on_own(k + 4, share)
+        if AHEAD <= k + 2 < STEPS - 1:
+            on_own(k + 2, hop)
+        if AHEAD <= k + 1 < STEPS - 1:
+            on_own(k + 1, pass_on)
         out_ref[k] = times(diag_ref[k])
         for i in range(k + 2, STEPS, 3):
             end_at = min(i + 3, STEPS)

time: 225 us -> 215 us (0.956); the launches traced: 224 us -> 210 us
  Pallas kernels: 223 us -> 209 us
    pallas_call x1, Pallas kernels: 223 us -> 209 us  [on_device(): pl.pallas_call(kernel, out_shape=jax.ShapeDtypeStruct(targets.shape, f32)...]
where the time goes in v4:
time: 215 us; the launch traced here: 210 us
  Pallas kernels  209 us (97%)
    pallas_call x1, Pallas kernels, on_device(): pl.pallas_call(kernel, out_shape=jax.ShapeDtypeStruct(targets.shape, f32)...  209 us

profile of v4, /device:TPU:24, one launch (start us, length us, event | category | flops | bytes accessed | tf_op | source)
XLA Modules:
  0.0 210.5 jit_solution(1587076367499214326)
XLA Ops:
  0.0 208.7 %shard_map.55 = f32[10,64,128]{2,1,0:T(8,128)} custom-call(f32[10,64,128]{2,1,0:T(8,128)} %target_ref.1, f32[64,3712]{1,0:T(8,128)} %bitcast.1, f32[10,64,1024]{2,1,0:T(8,128)} %diag_ref.1, f32[10,64,3712]{2,1,0:T(8,128)} %panel_ref.1, f32[45,64,1024]{2,1,0:T(8,128)} %below_ref.1), custom_call_target="tpu_custom_call" | custom-call | tf_op jit(solution)/shard_map/pallas_call | solution.py:515
  208.7 1.7 copy.7

commit v5 on v4

--- a/solution.py
+++ b/solution.py
@@ -398,19 +398,21 @@
     even = lax.rem(second, 2) == 0
     pair = jnp.where(even, second + 1, second - 1)
     other = wrap(pair + 2)
+    for j in range(2):
+        on_own(j, hop)
     panel_product(pair)
     give_zero(pair)
     give_one(second // 2)
-    for j in range(2):
+    for j in range(2, AHEAD):
         on_own(j, hop)
     panel_product(other)
     give_zero(other)
-    for j in range(2, AHEAD):
-        on_own(j, hop)
+    for j in range(2):
+        on_own(j, pass_on)
     for df in ORDER:
         last(df, FRONT)
     panel_half(wrap(second + 2), False)
-    for j in range(2):
+    for j in range(2, AHEAD):
         on_own(j, pass_on)
     for df in ORDER:
         last(df, BACK)
@@ -475,8 +477,6 @@
         arrive(k)
         own[k + 1] -= times(coupling(k, 0, 1))
         spread(k + 1)
-        if k + 2 < AHEAD:
-            on_own(k + 2, pass_on)
         if k == 0:
             for d in range(1, COLS):
                 term_copy(col, wrap(col + d, COLS), len(GROUPS) - 1).start()

time: 215 us -> 212 us (0.986)
  no operation moved by 1% of the time
where the time goes in v5:
time: 212 us; the launch traced here: 209 us
  Pallas kernels  207 us (98%)
    pallas_call x1, Pallas kernels, on_device(): pl.pallas_call(kernel, out_shape=jax.ShapeDtypeStruct(targets.shape, f32)...  207 us

profile of v5, /device:TPU:24, one launch (start us, length us, event | category | flops | bytes accessed | tf_op | source)
XLA Modules:
  0.0 209.2 jit_solution(15153157920404270819)
XLA Ops:
  0.0 207.5 %shard_map.55 = f32[10,64,128]{2,1,0:T(8,128)} custom-call(f32[10,64,128]{2,1,0:T(8,128)} %target_ref.1, f32[64,3712]{1,0:T(8,128)} %bitcast.1, f32[10,64,1024]{2,1,0:T(8,128)} %diag_ref.1, f32[10,64,3712]{2,1,0:T(8,128)} %panel_ref.1, f32[45,64,1024]{2,1,0:T(8,128)} %below_ref.1), custom_call_target="tpu_custom_call" | custom-call | tf_op jit(solution)/shard_map/pallas_call | solution.py:515
  207.5 1.7 copy.7
